TPU v7x, 32 devices: a whole 2x2x4 slice. The times are simulated.
32 devices in a mesh: grp: 2 (over x), node: 16 (over z, y, core).
Axes of the slice: x: 2, y: 2, z: 4, core: 2. Of those that a mesh axis runs over, the one named last changes fastest.
Arguments:
- queries: bfloat16 [32, 4, 16384], P(('grp', 'node')), parts along dimension 0, may hold values from -150 to 150
- shared_kv: bfloat16 [2, 24576, 1024], P(None, ('grp', 'node')), parts along dimension 1, may hold values from -12 to 12
- page_mask: int32 [192, 16], P(('grp', 'node')), parts along dimension 0, may hold values from 0 to 1, as said below
- slot_request: int32 [32], P('grp'), parts along dimension 0, may hold values from 0 to 15, each once
- suffix_blocks: int32 [32], P(('grp', 'node')), parts along dimension 0, may hold values from 1 to 2, as said below
- suffix_kv: bfloat16 [32, 2, 256, 1024], P(('grp', 'node')), parts along dimension 0, may hold values from -8 to 8
- new_kv: bfloat16 [32, 2, 4, 1024], P(('grp', 'node')), parts along dimension 0, may hold values from -12 to 12
Outputs:
- attn_out: bfloat16 [32, 4, 16384], P(('grp', 'node')), parts along dimension 0
There are 2 independent parts, one for each index of `grp`. A program takes and returns all parts, laid end to end along the dimension named above; each array names one. Nothing has to cross between parts.
Inputs may be any that keep to these rules, and one draw needn't show every extreme that they name: page_mask[p, r] is 1 for the 32 pages of the system prompt and for the 32 pages of the prefix of request r's group (2 groups, each request in one), else 0. `suffix_blocks`: some slot has exactly 2.
All inputs are finite; a program needn't handle non-finite values.
Results may differ from a plain program's by a relative error of at most 0.008.
Values may be sent and summed in bfloat16 or wider, within the bound.
A program may use at most 128 MiB of HBM per device.

v0:
```python
import jax
import jax.numpy as jnp
from jax import lax
from jax.sharding import PartitionSpec as P

H = 128
KVH = 8
DH = 128
BT = 128


MASKED_SCORE = -1e30


def normalized(outputs, totals):
    return (outputs / jnp.maximum(totals, 1.0)[..., None]).astype(jnp.bfloat16)


def suffix_part(queries, suffix_kv, suffix_blocks, new_kv):
    owned, step_count, _ = queries.shape
    group_size = H // KVH
    scaling = DH ** (-0.5)
    query_heads = queries.reshape(owned, step_count, KVH, group_size, DH)
    tokens = suffix_kv.shape[2]
    cached_keys = suffix_kv[:, 0].reshape(owned, tokens, KVH, DH)
    cached_values = suffix_kv[:, 1].reshape(owned, tokens, KVH, DH)
    recent_keys = new_kv[:, 0].reshape(owned, step_count, KVH, DH)
    recent_values = new_kv[:, 1].reshape(owned, step_count, KVH, DH)
    cached = (
        jnp.einsum(
            "bskgd,btkd->bskgt", query_heads, cached_keys, preferred_element_type=jnp.float32
        )
        * scaling
    )
    recent = (
        jnp.einsum(
            "bskgd,bjkd->bskgj", query_heads, recent_keys, preferred_element_type=jnp.float32
        )
        * scaling
    )
    live_pages = (jnp.arange(tokens) // BT)[None, :] < suffix_blocks[:, None]
    cached_allowed = live_pages[:, None, None, None, :]
    causal = jnp.arange(step_count)[None, :] <= jnp.arange(step_count)[:, None]
    recent_allowed = causal[None, :, None, None, :]
    cached = jnp.where(cached_allowed, cached, MASKED_SCORE)
    recent = jnp.where(recent_allowed, recent, MASKED_SCORE)
    set_max = jnp.maximum(jnp.max(cached, axis=-1), jnp.max(recent, axis=-1))
    cached_weights = jnp.where(cached_allowed, jnp.exp(cached - set_max[..., None]), 0.0)
    recent_weights = jnp.where(recent_allowed, jnp.exp(recent - set_max[..., None]), 0.0)
    totals = jnp.sum(cached_weights, axis=-1) + jnp.sum(recent_weights, axis=-1)
    outputs = jnp.einsum(
        "bskgt,btkd->bskgd",
        cached_weights.astype(jnp.bfloat16),
        cached_values,
        preferred_element_type=jnp.float32,
    )
    outputs = outputs + jnp.einsum(
        "bskgj,bjkd->bskgd",
        recent_weights.astype(jnp.bfloat16),
        recent_values,
        preferred_element_type=jnp.float32,
    )
    parts = normalized(outputs, totals)
    shape = (owned, step_count, H)
    return (set_max.reshape(shape), totals.reshape(shape), parts.reshape(owned, step_count, H * DH))


def shared_part(gathered, shared_kv, visible):
    slot_count, step_count, _ = gathered.shape
    group_size = H // KVH
    scaling = DH ** (-0.5)
    tokens = shared_kv.shape[1]
    page_count = tokens // BT
    key_rows = shared_kv[0].reshape(tokens, KVH, DH)
    value_rows = shared_kv[1].reshape(tokens, KVH, DH)
    per_block = 4

    def attend(query_block, allowed):
        scores = (
            jnp.einsum(
                "bskgd,tkd->bskgt", query_block, key_rows, preferred_element_type=jnp.float32
            )
            * scaling
        )
        scores = scores.reshape(per_block, step_count, KVH, group_size, page_count, BT)
        scores = jnp.where(allowed, scores, MASKED_SCORE)
        set_max = jnp.max(scores, axis=(-2, -1))
        weights = jnp.where(allowed, jnp.exp(scores - set_max[..., None, None]), 0.0)
        totals = jnp.sum(weights, axis=(-2, -1))
        weights = weights.astype(jnp.bfloat16).reshape(
            per_block, step_count, KVH, group_size, tokens
        )
        outputs = jnp.einsum(
            "bskgt,tkd->bskgd", weights, value_rows, preferred_element_type=jnp.float32
        )
        return (set_max, totals, normalized(outputs, totals))

    def one_block(block_index):
        query_block = lax.dynamic_slice_in_dim(gathered, block_index * per_block, per_block, 0)
        query_block = query_block.reshape(per_block, step_count, KVH, group_size, DH)
        page_flags = lax.dynamic_slice_in_dim(visible, block_index * per_block, per_block, 1)
        allowed = (page_flags.T > 0)[:, None, None, None, :, None]
        return attend(query_block, allowed)

    set_max, totals, parts = lax.map(one_block, jnp.arange(slot_count // per_block))
    shape = (slot_count, step_count, H)
    return (
        set_max.reshape(shape),
        totals.reshape(shape),
        parts.reshape(slot_count, step_count, H * DH),
    )


def finish(far_max, far_weight, far_numer, own_max, own_totals, own_parts):
    owned, step_count, _ = own_max.shape
    row_max = jnp.maximum(far_max, own_max)
    far_factor = jnp.exp(far_max - row_max)
    own_factor = jnp.exp(own_max - row_max) * own_totals
    numerator = far_numer.reshape(owned, step_count, H, DH) * far_factor[..., None]
    numerator = (
        numerator
        + own_parts.reshape(owned, step_count, H, DH).astype(jnp.float32) * own_factor[..., None]
    )
    denominator = far_weight * far_factor + own_factor
    result = (numerator / denominator[..., None]).reshape(owned, step_count, H * DH)
    return result.astype(jnp.bfloat16)


def per_device(queries, shared_kv, page_mask, slot_request, suffix_blocks, suffix_kv, new_kv):
    owned = queries.shape[0]
    step_count = queries.shape[1]
    gathered = lax.all_gather(queries, "node", axis=0, tiled=True)
    own_max, own_totals, own_parts = suffix_part(queries, suffix_kv, suffix_blocks, new_kv)
    slot_count = gathered.shape[0]
    selector = (jnp.arange(slot_count)[:, None] == slot_request[None, :]).astype(jnp.int32)
    visible = jnp.dot(page_mask, selector)
    part_max, part_totals, part_parts = shared_part(gathered, shared_kv, visible)
    maxima, totals = (
        lax.all_to_all(part_max, "node", split_axis=0, concat_axis=0, tiled=True),
        lax.all_to_all(part_totals, "node", split_axis=0, concat_axis=0, tiled=True),
    )
    received = lax.all_to_all(part_parts, "node", split_axis=0, concat_axis=0, tiled=True)
    sources = maxima.shape[0] // owned
    maxima = maxima.reshape(sources, owned, step_count, H)
    totals = totals.reshape(sources, owned, step_count, H)
    received = received.reshape(sources, owned, step_count, H, DH)
    far_max = jnp.max(maxima, axis=0)
    factor = jnp.exp(maxima - far_max) * totals
    far_numer = jnp.sum(factor[..., None] * received.astype(jnp.float32), axis=0).reshape(
        owned, step_count, H * DH
    )
    far_weight = jnp.sum(factor, axis=0)
    return finish(far_max, far_weight, far_numer, own_max, own_totals, own_parts)


def solution(mesh):
    placed = (
        P(("grp", "node"), None, None),
        P(None, ("grp", "node"), None),
        P(("grp", "node"), None),
        P("grp"),
        P(("grp", "node")),
        P(("grp", "node"), None, None, None),
        P(("grp", "node"), None, None, None),
    )
    return jax.shard_map(
        per_device,
        mesh=mesh,
        in_specs=placed,
        out_specs=P(("grp", "node"), None, None),
        check_vma=False,
    )
```

profile of v0, /device:TPU:13, one launch (start us, length us, event | category | flops | bytes accessed | tf_op | source)
XLA Modules:
  0.0 178.7 jit_solution(7347013587514343621)
XLA Ops:
  6.5 0.7 all-gather.2.cloned.1.call-update
  7.3 0.8 convolution_bitcast_fusion
  8.2 3.4 %fusion.71 = (bf16[1,768,1024]{2,1,0:T(8,128)(2,1)}, bf16[1,768,1024]{2,1,0:T(8,128)(2,1)S(1)}) fusion(bf16[2,768,1024]{2,1,0:T(8,128)(2,1)} %param.10), kind=kLoop, calls=%fused_computation.85 | loop fusion | bytes 6291456 | tf_op jit(solution)/shard_map/slice | solution.py:75
  11.5 0.7 copy.75
  12.2 0.9 copy.35
  13.1 1.7 copy.76
  14.9 1.6 copy.36
  16.5 34.2 %all-gather.2.cloned.1.call-done = bf16[16,4,16384]{2,1,0:T(4,128)(2,1)} async-done(((bf16[1,4,16384]{2,1,0:T(4,128)(2,1)}), bf16[16,4,16384]{2,1,0:T(4,128)(2,1)}) %all-gather.2.cloned.1.call-update) | async-done | bytes 2097168 | tf_op jit(solution)/shard_map/all_gather | solution.py:132
  50.6 40.6 %while.14 = (s32[]{:T(128)}, f32[4,4,4,8,16]{4,3,2,1,0:T(8,128)S(1)}, f32[4,4,4,8,16]{4,3,2,1,0:T(8,128)}, bf16[4,4,4,8,16,128]{5,4,3,2,1,0:T(8,128)(2,1)}, s32[...) while((s32[]{:T(128)}, ...), condition=%wide.region_3.4_spmd, body=%wide.region_0.3_spmd.sunk | while | flops 826275840 | bytes 32844156 | solution.py:105
  50.6 0.6 dynamic_slice.19
  51.9 1.2 constant_dynamic-slice_fusion.2
  53.7 1.2 bitcast_reduce_fusion.2
  55.0 1.9 %fusion.86 = f32[4,4,8,16]{3,1,0,2:T(4,128)S(1)} fusion(f32[8,4,4,16,768]{4,3,2,1,0:T(8,128)S(1)} %get-tuple-element.180, f32[4,4,8,16]{3,1,0,2:T(4,128)S(1)} %get-tuple-element.181, pred[4,768]{1,0:T(4,128)(4,1)S(1)} %bitcast.169), kind=kLoop, calls=%fused_computation.6.clone.1 | loop fusion | flops 7862272 | bytes 6310912 | tf_op jit(solution)/shard_map/while/body/eval_jaxpr/reduce_sum | solution.py:89
  56.9 0.7 copy_dynamic-update-slice_fusion.5
  57.6 2.3 %fusion.87 = bf16[1,4,4,8,16,128]{5,4,2,1,3,0:T(8,128)(2,1)S(1)} fusion(bf16[768,8,128]{2,0,1:T(8,128)(2,1)S(1)} %copy-done.1, f32[8,4,4,16,768]{4,3,2,1,0:T(8,128)S(1)} %get-tuple-element.180, f32[4,4,8,16]{3,1,0,2:T(4,128)S(1)} %get-tuple-element.181, pred[4,768]{1,0:T(4,128)(4,1)S(1)} %bitcast.170, f32[4,4,8,16]{3,1,0,2:T(4,128)S(1)} %broadcast_maximum_fusion.3), kind=kOutput, calls=%fused_computation.15.clone.1 | convolution fusion | flops 411041792 | bytes 8408064 | tf_op jit(solution)/shard_map/while/body/eval_jaxpr/bskgt,tkd->bskgd/dot_general | solution.py:93
  59.9 0.9 copy_dynamic-update-slice_fusion.6
  62.1 1.2 constant_dynamic-slice_fusion.2
  63.9 1.2 bitcast_reduce_fusion.2
  65.1 1.9 %fusion.86 = f32[4,4,8,16]{3,1,0,2:T(4,128)S(1)} fusion(f32[8,4,4,16,768]{4,3,2,1,0:T(8,128)S(1)} %get-tuple-element.180, f32[4,4,8,16]{3,1,0,2:T(4,128)S(1)} %get-tuple-element.181, pred[4,768]{1,0:T(4,128)(4,1)S(1)} %bitcast.169), kind=kLoop, calls=%fused_computation.6.clone.1 | loop fusion | flops 7862272 | bytes 6310912 | tf_op jit(solution)/shard_map/while/body/eval_jaxpr/reduce_sum | solution.py:89
  67.1 0.7 copy_dynamic-update-slice_fusion.5
  67.8 2.3 %fusion.87 = bf16[1,4,4,8,16,128]{5,4,2,1,3,0:T(8,128)(2,1)S(1)} fusion(bf16[768,8,128]{2,0,1:T(8,128)(2,1)S(1)} %copy-done.1, f32[8,4,4,16,768]{4,3,2,1,0:T(8,128)S(1)} %get-tuple-element.180, f32[4,4,8,16]{3,1,0,2:T(4,128)S(1)} %get-tuple-element.181, pred[4,768]{1,0:T(4,128)(4,1)S(1)} %bitcast.170, f32[4,4,8,16]{3,1,0,2:T(4,128)S(1)} %broadcast_maximum_fusion.3), kind=kOutput, calls=%fused_computation.15.clone.1 | convolution fusion | flops 411041792 | bytes 8408064 | tf_op jit(solution)/shard_map/while/body/eval_jaxpr/bskgt,tkd->bskgd/dot_general | solution.py:93
  70.1 0.9 copy_dynamic-update-slice_fusion.6
  72.3 1.2 constant_dynamic-slice_fusion.2
  74.0 1.2 bitcast_reduce_fusion.2
  75.3 1.9 %fusion.86 = f32[4,4,8,16]{3,1,0,2:T(4,128)S(1)} fusion(f32[8,4,4,16,768]{4,3,2,1,0:T(8,128)S(1)} %get-tuple-element.180, f32[4,4,8,16]{3,1,0,2:T(4,128)S(1)} %get-tuple-element.181, pred[4,768]{1,0:T(4,128)(4,1)S(1)} %bitcast.169), kind=kLoop, calls=%fused_computation.6.clone.1 | loop fusion | flops 7862272 | bytes 6310912 | tf_op jit(solution)/shard_map/while/body/eval_jaxpr/reduce_sum | solution.py:89
  77.2 0.7 copy_dynamic-update-slice_fusion.5
  77.9 2.3 %fusion.87 = bf16[1,4,4,8,16,128]{5,4,2,1,3,0:T(8,128)(2,1)S(1)} fusion(bf16[768,8,128]{2,0,1:T(8,128)(2,1)S(1)} %copy-done.1, f32[8,4,4,16,768]{4,3,2,1,0:T(8,128)S(1)} %get-tuple-element.180, f32[4,4,8,16]{3,1,0,2:T(4,128)S(1)} %get-tuple-element.181, pred[4,768]{1,0:T(4,128)(4,1)S(1)} %bitcast.170, f32[4,4,8,16]{3,1,0,2:T(4,128)S(1)} %broadcast_maximum_fusion.3), kind=kOutput, calls=%fused_computation.15.clone.1 | convolution fusion | flops 411041792 | bytes 8408064 | tf_op jit(solution)/shard_map/while/body/eval_jaxpr/bskgt,tkd->bskgd/dot_general | solution.py:93
  80.2 0.8 copy_dynamic-update-slice_fusion.6
  82.4 1.2 constant_dynamic-slice_fusion.2
  84.2 1.2 bitcast_reduce_fusion.2
  85.4 1.9 %fusion.86 = f32[4,4,8,16]{3,1,0,2:T(4,128)S(1)} fusion(f32[8,4,4,16,768]{4,3,2,1,0:T(8,128)S(1)} %get-tuple-element.180, f32[4,4,8,16]{3,1,0,2:T(4,128)S(1)} %get-tuple-element.181, pred[4,768]{1,0:T(4,128)(4,1)S(1)} %bitcast.169), kind=kLoop, calls=%fused_computation.6.clone.1 | loop fusion | flops 7862272 | bytes 6310912 | tf_op jit(solution)/shard_map/while/body/eval_jaxpr/reduce_sum | solution.py:89
  87.4 0.7 copy_dynamic-update-slice_fusion.5
  88.1 2.3 %fusion.87 = bf16[1,4,4,8,16,128]{5,4,2,1,3,0:T(8,128)(2,1)S(1)} fusion(bf16[768,8,128]{2,0,1:T(8,128)(2,1)S(1)} %copy-done.1, f32[8,4,4,16,768]{4,3,2,1,0:T(8,128)S(1)} %get-tuple-element.180, f32[4,4,8,16]{3,1,0,2:T(4,128)S(1)} %get-tuple-element.181, pred[4,768]{1,0:T(4,128)(4,1)S(1)} %bitcast.170, f32[4,4,8,16]{3,1,0,2:T(4,128)S(1)} %broadcast_maximum_fusion.3), kind=kOutput, calls=%fused_computation.15.clone.1 | convolution fusion | flops 411041792 | bytes 8408064 | tf_op jit(solution)/shard_map/while/body/eval_jaxpr/bskgt,tkd->bskgd/dot_general | solution.py:93
  90.4 0.9 copy_dynamic-update-slice_fusion.6
  91.3 1.7 reshape.360
  93.0 5.7 %all-to-all-start.1 = ((f32[16,4,128]{2,1,0:T(4,128)}), f32[16,4,128]{2,1,0:T(4,128)S(1)}, u32[]{:S(2)}, u32[]{:S(2)}) async-start(f32[16,4,128]{2,1,0:T(4,128)} %reshape.360), calls=%async_computation.1 | async-start | bytes 65536 | tf_op jit(solution)/shard_map/all_to_all | solution.py:140
  98.7 0.7 reshape.359
  99.4 3.4 %all-to-all-done.1 = f32[16,4,128]{2,1,0:T(4,128)S(1)} async-done(((f32[16,4,128]{2,1,0:T(4,128)}), f32[16,4,128]{2,1,0:T(4,128)S(1)}, u32[]{:S(2)}, u32[]{:S(2)}) %all-to-all-start.1) | async-done | bytes 32800 | tf_op jit(solution)/shard_map/all_to_all | solution.py:140
  102.8 5.9 %all-to-all-start = ((f32[16,4,128]{2,1,0:T(4,128)}), f32[16,4,128]{2,1,0:T(4,128)S(1)}, u32[]{:S(2)}, u32[]{:S(2)}) async-start(f32[16,4,128]{2,1,0:T(4,128)} %reshape.359), calls=%async_computation | async-start | bytes 65536 | tf_op jit(solution)/shard_map/all_to_all | solution.py:139
  108.7 4.1 %reshape.361 = bf16[16,4,16384]{2,1,0:T(4,128)(2,1)} reshape(bf16[4,4,4,8,16,128]{5,4,3,2,1,0:T(8,128)(2,1)} %get-tuple-element.56) | data formatting | bytes 4194304 | tf_op jit(solution)/shard_map/reshape | solution.py:110
  112.9 6.1 %all-to-all-start.2 = ((bf16[16,4,16384]{2,1,0:T(4,128)(2,1)}), bf16[16,4,16384]{2,1,0:T(4,128)(2,1)S(1)}, u32[]{:S(2)}, u32[]{:S(2)}) async-start(bf16[16,4,16384]{2,1,0:T(4,128)(2,1)} %reshape.361), calls=%async_computation.2 | async-start | bytes 4194304 | tf_op jit(solution)/shard_map/all_to_all | solution.py:142
  119.0 2.1 %fusion.72 = (bf16[1,1,256,1024]{3,2,1,0:T(8,128)(2,1)}, bf16[1,1,256,1024]{3,2,1,0:T(8,128)(2,1)S(1)}) fusion(bf16[1,2,256,1024]{3,2,1,0:T(8,128)(2,1)} %param.14), kind=kLoop, calls=%fused_computation.86 | loop fusion | bytes 2097152 | tf_op jit(solution)/shard_map/slice | solution.py:26
  123.4 1.2 copy.78
  125.4 2.6 %mul.113 = f32[16,4,128,128]{3,2,1,0:T(8,128)} broadcast(f32[16,4,128]{2,1,0:T(4,128)S(1)} %get-tuple-element.108), dimensions={0,1,2} | broadcast | bytes 4227072 | tf_op jit(solution)/shard_map/mul | solution.py:149
  128.0 5.6 %mul.114 = f32[16,4,16384]{2,1,0:T(4,128)} reshape(f32[16,4,128,128]{3,2,1,0:T(8,128)} %mul.113) | data formatting | bytes 8388608 | tf_op jit(solution)/shard_map/mul | solution.py:149
  133.6 32.9 %all-to-all-done.2 = bf16[16,4,16384]{2,1,0:T(4,128)(2,1)S(1)} async-done(((bf16[16,4,16384]{2,1,0:T(4,128)(2,1)}), bf16[16,4,16384]{2,1,0:T(4,128)(2,1)S(1)}, u32[]{:S(2)}, u32[]{:S(2)}) %all-to-all-start.2) | async-done | bytes 2097184 | tf_op jit(solution)/shard_map/all_to_all | solution.py:142
  166.5 3.6 %multiply_reduce_fusion = f32[4,16384]{1,0:T(4,128)S(1)} fusion(f32[16,4,16384]{2,1,0:T(4,128)} %mul.114, bf16[16,4,16384]{2,1,0:T(4,128)(2,1)S(1)} %all-to-all-done.2), kind=kLoop, calls=%fused_computation.29 | loop fusion | flops 3080192 | bytes 6553600 | tf_op jit(solution)/shard_map/reduce_sum | solution.py:149
  171.0 0.8 copy.52
  (68 shorter events, 7.9 us)
Async XLA Ops:
  6.5 0.8 copy-start
  6.5 44.1 %all-gather.2.cloned.1.call-start = ((), (), s32[]{:S(2)}) async-start(), calls=%async_computation.3 | async-start | bytes 2228224 | tf_op jit(solution)/shard_map/all_gather | solution.py:132
  54.9 2.7 %copy-start.1 = (bf16[768,8,128]{2,0,1:T(8,128)(2,1)S(1)}, bf16[768,8,128]{2,0,1:T(8,128)(2,1)}, u32[]{:S(2)}) copy-start(bf16[768,8,128]{2,0,1:T(8,128)(2,1)} %get-tuple-element.218) | copy-start | bytes 4718596 | tf_op jit(solution)/shard_map/while
  65.1 2.6 %copy-start.1 = (bf16[768,8,128]{2,0,1:T(8,128)(2,1)S(1)}, bf16[768,8,128]{2,0,1:T(8,128)(2,1)}, u32[]{:S(2)}) copy-start(bf16[768,8,128]{2,0,1:T(8,128)(2,1)} %get-tuple-element.218) | copy-start | bytes 4718596 | tf_op jit(solution)/shard_map/while
  75.3 2.6 %copy-start.1 = (bf16[768,8,128]{2,0,1:T(8,128)(2,1)S(1)}, bf16[768,8,128]{2,0,1:T(8,128)(2,1)}, u32[]{:S(2)}) copy-start(bf16[768,8,128]{2,0,1:T(8,128)(2,1)} %get-tuple-element.218) | copy-start | bytes 4718596 | tf_op jit(solution)/shard_map/while
  85.4 2.7 %copy-start.1 = (bf16[768,8,128]{2,0,1:T(8,128)(2,1)S(1)}, bf16[768,8,128]{2,0,1:T(8,128)(2,1)}, u32[]{:S(2)}) copy-start(bf16[768,8,128]{2,0,1:T(8,128)(2,1)} %get-tuple-element.218) | copy-start | bytes 4718596 | tf_op jit(solution)/shard_map/while
  93.0 9.9 %all-to-all-start.1 = ((f32[16,4,128]{2,1,0:T(4,128)}), f32[16,4,128]{2,1,0:T(4,128)S(1)}, u32[]{:S(2)}, u32[]{:S(2)}) async-start(f32[16,4,128]{2,1,0:T(4,128)} %reshape.360), calls=%async_computation.1 | async-start | bytes 65536 | tf_op jit(solution)/shard_map/all_to_all | solution.py:140
  102.8 10.1 %all-to-all-start = ((f32[16,4,128]{2,1,0:T(4,128)}), f32[16,4,128]{2,1,0:T(4,128)S(1)}, u32[]{:S(2)}, u32[]{:S(2)}) async-start(f32[16,4,128]{2,1,0:T(4,128)} %reshape.359), calls=%async_computation | async-start | bytes 65536 | tf_op jit(solution)/shard_map/all_to_all | solution.py:139
  112.8 8.5 %copy-start.2 = (bf16[1,4,16384]{2,1,0:T(4,128)(2,1)S(1)}, bf16[1,4,16384]{2,1,0:T(4,128)(2,1)}, u32[]{:S(2)}) copy-start(bf16[1,4,16384]{2,1,0:T(4,128)(2,1)} %param.9) | copy-start | bytes 393220
  112.8 9.2 %copy-start.3 = (bf16[1,2,4,1024]{3,2,1,0:T(4,128)(2,1)S(1)}, bf16[1,2,4,1024]{3,2,1,0:T(4,128)(2,1)}, u32[]{:S(2)}) copy-start(bf16[1,2,4,1024]{3,2,1,0:T(4,128)(2,1)} %param.15) | copy-start | bytes 49156
  112.9 53.6 %all-to-all-start.2 = ((bf16[16,4,16384]{2,1,0:T(4,128)(2,1)}), bf16[16,4,16384]{2,1,0:T(4,128)(2,1)S(1)}, u32[]{:S(2)}, u32[]{:S(2)}) async-start(bf16[16,4,16384]{2,1,0:T(4,128)(2,1)} %reshape.361), calls=%async_computation.2 | async-start | bytes 4194304 | tf_op jit(solution)/shard_map/all_to_all | solution.py:142
Sparse Core Ops, SparseCore 0:
  9.5 41.0 all-gather.1
where the time goes:
time: 180 us; the launch traced here: 179 us
  waiting for transfers between devices  71.3 us (40%)
  local copies, waits for them, and re-layouts  43.9 us (24%)
  starting transfers between devices  17.7 us (10%)
  matrix products  16.3 us (9%)
  between operations  14.2 us (8%)
  other arithmetic  12.6 us (7%)
  loops' own time  2.73 us (2%)
    all_gather x1, waiting for transfers between devices, per_device(): gathered = lax.all_gather(queries, 'node', axis=0, tiled=True)  34.2 us
    all_to_all x1, waiting for transfers between devices, per_device(): lax.all_to_all(part_parts, 'node', split_axis=0, concat_axis=0, tiled=True)  32.9 us
    dot_general x4, matrix products, attend(): jnp.einsum('bskgt,tkd->bskgd', weights, value_rows, preferred_element_typ...  9.21 us
    mul x2, local copies, waits for them, and re-layouts, per_device(): factor[..., None] * received.astype(jnp.float32)  8.17 us
    reduce_sum x4, other arithmetic, attend(): totals = jnp.sum(weights, axis=(-2, -1))  7.8 us
    all_to_all x1, starting transfers between devices, per_device(): lax.all_to_all(part_parts, 'node', split_axis=0, concat_axis=0, tiled=True)  6.12 us
    dynamic_update_slice x8, local copies, waits for them, and re-layouts, shared_part(): lax.map(one_block, jnp.arange(slot_count // per_block))  6.11 us
    all_to_all x1, starting transfers between devices, per_device(): lax.all_to_all(part_max, 'node', split_axis=0, concat_axis=0, tiled=True)  5.89 us
  transfers between devices with their start and end apart: 4, of which 4 were waited for; matrix products, arithmetic and copies ran while one was open for 16% of the time, Pallas kernels for 0%

commit v1 on v0

v1 whole, which is shorter than its diff:
```python
import functools

import jax
import jax.numpy as jnp
import numpy as np
from jax import lax
from jax.experimental import pallas as pl
from jax.experimental.pallas import tpu as pltpu
from jax.sharding import PartitionSpec as P

H = 128
KVH = 8
DH = 128
BT = 128
STEPS = 4
G = H // KVH
HALF = KVH // 2
ROWS = STEPS * G
LANES = 2 * ROWS
SCALE2 = float(DH ** (-0.5) * np.log2(np.e))
BIG = 1e30
F32 = jnp.float32
BF16 = jnp.bfloat16
NT = (((1,), (1,)), ((), ()))


def merge(o1, l1, o2, l2):
    top = jnp.maximum(l1, l2)
    a, b = jnp.exp2(l1 - top), jnp.exp2(l2 - top)
    both = a + b
    inv = 1.0 / both
    return o1 * (a * inv) + o2 * (b * inv), top + jnp.log2(both)


def attend(q, segments):
    scores, top = [], None
    for keys, _, penalty in segments:
        s = lax.dot_general(keys, q, NT, preferred_element_type=F32)
        scores.append(s)
        if penalty.shape[0] == 1:
            m = jnp.max(s, axis=0, keepdims=True) - penalty
        else:
            m = jnp.max(s - penalty, axis=0, keepdims=True)
        top = m if top is None else jnp.maximum(top, m)
    out, total = None, None
    for s, (_, values, penalty) in zip(scores, segments):
        w = jnp.exp2((s - jnp.where(penalty > 0, BIG, top)) * SCALE2)
        t = jnp.sum(w, axis=0, keepdims=True)
        o = jnp.dot(values, w.astype(BF16), preferred_element_type=F32)
        total = t if total is None else total + t
        out = o if out is None else out + o
    live = total > 0
    inv = 1.0 / jnp.where(live, total, 1.0)
    lse = jnp.where(live, top * SCALE2 + jnp.log2(jnp.where(live, total, 1.0)), -BIG)
    return out * inv, lse


def kernel(
    chips, tokens, q_ref, kv_ref, suf_ref, new_ref, bias_ref, out_ref,
    qb, kvs, sufs, news, bias, vt, svt, part_o, part_l, rs_in, rs_out, rl_in, rl_out, fin, land,
    loc_sem, sib_send, sib_recv, g_send, g_recv, o_send, o_recv, l_send, l_recv, f_send, f_recv,
):
    half = chips // 2
    node = lax.axis_index("node")
    core, chip = lax.rem(node, 2), lax.div(node, 2)
    odd, pair_no = lax.rem(chip, 2), lax.div(chip, 2)
    pos = (1 - odd) * pair_no + odd * (chips - 1 - pair_no)

    def at(position):
        back = lax.div(position, half)
        place = (1 - back) * 2 * position + back * (2 * (chips - 1 - position) + 1)
        return {"node": place * 2 + core}

    sibling = {"node": node + 1 - 2 * core}
    ahead = (at(lax.rem(pos + 1, chips)), at(lax.rem(pos + chips - 1, chips)))
    pages = tokens // BT

    def behind(d, k):
        return lax.rem(pos + chips - k, chips) if d == 0 else lax.rem(pos + k, chips)

    mine = pl.multiple_of(core * HALF * DH, HALF * DH)
    theirs = pl.multiple_of((1 - core) * HALF * DH, HALF * DH)
    slot_rows = pl.ds(pl.multiple_of(core * ROWS, ROWS), ROWS)

    def views(columns, heads):
        return (
            (q_ref.at[pl.ds(heads, HALF)], qb.at[pos, :, slot_rows, :]),
            (bias_ref, bias.at[core]),
            (kv_ref.at[:, :, pl.ds(columns, HALF * DH)], kvs.at[:, core]),
            (suf_ref.at[:, :, pl.ds(columns, HALF * DH)], sufs.at[:, core]),
            (new_ref.at[:, :, pl.ds(columns, HALF * DH)], news.at[:, core]),
        )

    local = [
        pltpu.make_async_copy(src, dst, loc_sem.at[i])
        for i, (src, dst) in enumerate(views(mine, core * HALF))
    ]
    across = [
        pltpu.make_async_remote_copy(
            src_ref=src, dst_ref=dst, send_sem=sib_send.at[i], recv_sem=sib_recv.at[i],
            device_id=sibling,
        )
        for i, (src, dst) in enumerate(views(theirs, (1 - core) * HALF))
    ]

    def hop(d, h, piece):
        ref = qb.at[behind(d, h - 1), pl.ds(2 * piece, 2)]
        return pltpu.make_async_remote_copy(
            src_ref=ref, dst_ref=ref, send_sem=g_send.at[d, h, piece],
            recv_sem=g_recv.at[d, h, piece], device_id=ahead[d],
        )

    def landed(d, h, piece):
        ref = qb.at[behind(d, h), pl.ds(2 * piece, 2)]
        return pltpu.make_async_remote_copy(
            src_ref=ref, dst_ref=ref, send_sem=g_send.at[d, h, piece],
            recv_sem=g_recv.at[d, h, piece], device_id=ahead[d],
        )

    def stage(d, j, piece):
        heads = pl.ds(2 * piece, 2)
        return (
            pltpu.make_async_remote_copy(
                src_ref=rs_out.at[d, j, heads], dst_ref=rs_in.at[d, j, heads],
                send_sem=o_send.at[d, j, piece], recv_sem=o_recv.at[d, j, piece],
                device_id=ahead[d],
            ),
            pltpu.make_async_remote_copy(
                src_ref=rl_out.at[d, j, piece], dst_ref=rl_in.at[d, j, piece],
                send_sem=l_send.at[d, j, piece], recv_sem=l_recv.at[d, j, piece],
                device_id=ahead[d],
            ),
        )

    for copy in local:
        copy.start()
    barrier = pltpu.get_barrier_semaphore()
    for other in (sibling, *ahead):
        pl.semaphore_signal(barrier, inc=1, device_id=other)
    pl.semaphore_wait(barrier, 3)
    for copy in across:
        copy.start()
    local[0].wait()
    across[0].wait_recv()
    for piece in range(2):
        for d in range(2):
            hop(d, 1, piece).start()
    for copy in local[1:]:
        copy.wait()
    for copy in across[1:]:
        copy.wait_recv()

    def columns_of(k):
        return pl.ds(pl.multiple_of(k * DH, DH), DH)

    @pl.loop(0, HALF)
    def _(k):
        for s in range(2):
            vt[k, s] = kvs[1, s, :, columns_of(k)].T
            svt[k, s] = sufs[1, s, :, columns_of(k)].T

    def shared_segments(k, blocks):
        found = []
        for s in range(2):
            for page in range(pages):
                rows = slice(page * BT, (page + 1) * BT)
                penalty = jnp.concatenate([bias[s, b, page : page + 1, :] for b in blocks], axis=1)
                found.append((kvs[0, s, rows, columns_of(k)], vt[k, s, :, rows], penalty))
        return found

    def keep(block, k, o, lse):
        part_o[block, k] = o
        part_l[block, k] = lse

    def own_block():
        token = lax.broadcasted_iota(jnp.int32, (16, LANES), 0)
        lane = lax.broadcasted_iota(jnp.int32, (16, LANES), 1)
        step = lax.rem(lax.div(lane, G), STEPS)

        @pl.loop(0, HALF)
        def _(k):
            found = shared_segments(k, [pos])
            for s in range(2):
                for page in range(sufs.shape[2] // BT):
                    rows = slice(page * BT, (page + 1) * BT)
                    penalty = bias[s, chips, page : page + 1, :]
                    found.append((sufs[0, s, rows, columns_of(k)], svt[k, s, :, rows], penalty))
                seen = (token <= step) & (lax.div(lane, ROWS) == s)
                found.append(
                    (
                        news[0, s, :, columns_of(k)],
                        news[1, s, :, columns_of(k)].T,
                        jnp.where(seen, 0.0, BIG),
                    )
                )
            keep(pos, k, *attend(qb[pos, k], found))

    def one_block(block):
        @pl.loop(0, HALF)
        def _(k):
            keep(block, k, *attend(qb[block, k], shared_segments(k, [block])))

    def two_blocks(a, b):
        @pl.loop(0, HALF)
        def _(k):
            q = jnp.concatenate([qb[a, k], qb[b, k]], axis=0)
            o, lse = attend(q, shared_segments(k, [a, b]))
            keep(a, k, o[:, :LANES], lse[:, :LANES])
            keep(b, k, o[:, LANES:], lse[:, LANES:])

    def pass_on(h):
        for piece in range(2):
            for d in range(2):
                landed(d, h, piece).wait_recv()

                @pl.when((h + 1 < half) | (d == piece))
                def _():
                    hop(d, h + 1, piece).start()

    pass_on(1)
    own_block()

    @pl.loop(2, half + 1)
    def _(h):
        @pl.when(h < half)
        def _():
            pass_on(h)

        @pl.when(h == half)
        def _():
            for d in range(2):
                landed(d, half, d).wait_recv()
            far = behind(0, half)
            one_block(far)
            for d in range(2):
                for i in range(2):
                    k = 2 * d + i
                    rs_out[d, 1, k] = part_o[far, k].astype(BF16)
                    rl_out[d, 1, d, i : i + 1, :] = part_l[far, k]
                for copy in stage(d, 1, d):
                    copy.start()

        two_blocks(behind(0, h - 1), behind(1, h - 1))

    def incoming(d, j, piece):
        for copy in stage(d, j, piece):
            copy.wait_recv()

    def received(d, j, k):
        return rs_in[d, j, k].astype(F32), rl_in[d, j, k // 2, k % 2 : k % 2 + 1, :]

    @pl.loop(2, half + 1)
    def _(j):
        for piece in range(2):
            for d in range(2):
                target = behind(1 - d, half + 1 - j)

                def add():
                    incoming(d, j - 1, piece)
                    for k in (2 * piece, 2 * piece + 1):
                        o, lse = merge(*received(d, j - 1, k), part_o[target, k], part_l[target, k])
                        rs_out[d, j, k] = o.astype(BF16)
                        rl_out[d, j, piece, k % 2 : k % 2 + 1, :] = lse

                def begin():
                    for k in (2 * piece, 2 * piece + 1):
                        rs_out[d, j, k] = part_o[target, k].astype(BF16)
                        rl_out[d, j, piece, k % 2 : k % 2 + 1, :] = part_l[target, k]

                if d == piece:
                    add()
                else:
                    pl.when(j > 2)(add)
                    pl.when(j == 2)(begin)
                for copy in stage(d, j, piece):
                    copy.start()

    for piece in range(2):
        for d in range(2):
            incoming(d, half, piece)
        for k in (2 * piece, 2 * piece + 1):
            o, lse = merge(*received(0, half, k), part_o[pos, k], part_l[pos, k])
            o, _ = merge(o, lse, *received(1, half, k))
            fin[k] = o.T.astype(BF16)
    sib_rows = pl.ds(pl.multiple_of((1 - core) * ROWS, ROWS), ROWS)
    give = pltpu.make_async_remote_copy(
        src_ref=fin.at[:, sib_rows, :], dst_ref=land, send_sem=f_send, recv_sem=f_recv,
        device_id=sibling,
    )
    give.start()
    out_ref[pl.ds(core * HALF, HALF)] = fin[:, slot_rows, :]
    give.wait_recv()
    out_ref[pl.ds((1 - core) * HALF, HALF)] = land[...]
    give.wait_send()
    for copy in across:
        copy.wait_send()

    @pl.loop(1, half + 1)
    def _(h):
        for piece in range(2):
            for d in range(2):
                @pl.when((h < half) | (d == piece))
                def _():
                    hop(d, h, piece).wait_send()

                @pl.when((h > 1) | (d == piece))
                def _():
                    for copy in stage(d, h, piece):
                        copy.wait_send()


def ring_order(chips):
    return np.array([2 * r if r < chips // 2 else 2 * (chips - 1 - r) + 1 for r in range(chips)])


def per_device(queries, shared_kv, page_mask, slot_request, suffix_blocks, suffix_kv, new_kv):
    nodes = lax.axis_size("node")
    chips = nodes // 2
    half = chips // 2
    tokens = shared_kv.shape[1]
    suffix_tokens = suffix_kv.shape[2]
    core = lax.rem(lax.axis_index("node"), 2)

    q = queries.reshape(STEPS, KVH, G, DH).transpose(1, 0, 2, 3).reshape(KVH, ROWS, DH)
    new = jnp.pad(new_kv[0], ((0, 0), (0, 16 - STEPS), (0, 0)))
    selector = (slot_request[:, None] == jnp.arange(page_mask.shape[1])[None, :])
    visible = jnp.sum(
        jnp.where(selector[None], page_mask[:, None, :], 0), axis=-1
    )
    blocks = visible.reshape(-1, chips, 2)[:, ring_order(chips), :].transpose(1, 0, 2)
    suffix_live = (jnp.arange(blocks.shape[1]) < suffix_blocks[0])[:, None] & (
        jnp.arange(2) == core
    )[None, :]
    allowed = jnp.concatenate([blocks > 0, suffix_live[None]], axis=0)
    bias = jnp.where(allowed, 0.0, BIG).astype(F32)
    bias = jnp.repeat(bias, ROWS, axis=-1)
    bias = jnp.pad(bias, ((0, 0), (0, -bias.shape[1] % 8), (0, 0)))

    dma = pltpu.SemaphoreType.DMA
    grid_sems = dma((2, half + 1, 2))
    out = pl.pallas_call(
        functools.partial(kernel, chips, tokens),
        out_shape=jax.ShapeDtypeStruct((KVH, ROWS, DH), BF16),
        in_specs=[pl.BlockSpec(memory_space=pl.ANY)] * 5,
        out_specs=pl.BlockSpec(memory_space=pltpu.VMEM),
        scratch_shapes=[
            pltpu.VMEM((chips, HALF, LANES, DH), BF16),
            pltpu.VMEM((2, 2, tokens, HALF * DH), BF16),
            pltpu.VMEM((2, 2, suffix_tokens, HALF * DH), BF16),
            pltpu.VMEM((2, 2, 16, HALF * DH), BF16),
            pltpu.VMEM((2,) + bias.shape, F32),
            pltpu.VMEM((HALF, 2, DH, tokens), BF16),
            pltpu.VMEM((HALF, 2, DH, suffix_tokens), BF16),
            pltpu.VMEM((chips, HALF, DH, LANES), F32),
            pltpu.VMEM((chips, HALF, 1, LANES), F32),
            pltpu.VMEM((2, half + 1, HALF, DH, LANES), BF16),
            pltpu.VMEM((2, half + 1, HALF, DH, LANES), BF16),
            pltpu.VMEM((2, half + 1, 2, 8, LANES), F32),
            pltpu.VMEM((2, half + 1, 2, 8, LANES), F32),
            pltpu.VMEM((HALF, LANES, DH), BF16),
            pltpu.VMEM((HALF, ROWS, DH), BF16),
            dma((5,)), dma((5,)), dma((5,)),
            grid_sems, grid_sems, grid_sems, grid_sems, grid_sems, grid_sems,
            dma, dma,
        ],
        compiler_params=pltpu.CompilerParams(
            collective_id=0, has_side_effects=True, vmem_limit_bytes=56 * 1024 * 1024
        ),
    )(q, shared_kv, suffix_kv[0], new, bias)
    out = out.reshape(KVH, STEPS, G, DH).transpose(1, 0, 2, 3)
    return out.reshape(1, STEPS, H * DH)


def solution(mesh):
    placed = (
        P(("grp", "node"), None, None),
        P(None, ("grp", "node"), None),
        P(("grp", "node"), None),
        P("grp"),
        P(("grp", "node")),
        P(("grp", "node"), None, None, None),
        P(("grp", "node"), None, None, None),
    )
    return jax.shard_map(
        per_device,
        mesh=mesh,
        in_specs=placed,
        out_specs=P(("grp", "node"), None, None),
        check_vma=False,
    )
```

time: 180 us -> 59.4 us (0.33)
  the two profiles are of different devices: /device:TPU:13 before, /device:TPU:0 now
where the time goes in v1:
time: 59.4 us; the launch traced here: 59.1 us
  Pallas kernels  49.7 us (84%)
  local copies, waits for them, and re-layouts  6.27 us (11%)
  other arithmetic  2.44 us (4%)
  between operations  0.7 us (1%)
    pallas_call x1, Pallas kernels, per_device(): pl.pallas_call(functools.partial(kernel, chips, tokens), out_shape=jax.Sh...  49.7 us
    pad x1, local copies, waits for them, and re-layouts, per_device(): new = jnp.pad(new_kv[0], ((0, 0), (0, 16 - STEPS), (0, 0)))  1.34 us

profile of v1, /device:TPU:0, one launch (start us, length us, event | category | flops | bytes accessed | tf_op | source)
XLA Modules:
  0.0 59.1 jit_solution(11394928003813137722)
XLA Ops:
  0.7 0.1 broadcast_and_fusion
  0.8 0.7 %iota_compare_fusion = pred[16,16]{1,0:T(8,128)(4,1)S(1)} fusion(s32[16]{0:T(128)} %param.12), kind=kLoop, calls=%fused_computation.2 | loop fusion | flops 256 | bytes 320 | tf_op jit(solution)/shard_map/eq | solution.py:326
  1.5 0.9 %select_reduce_fusion = s32[6,16]{1,0:T(8,128)S(1)} fusion(s32[6,16]{1,0:T(8,128)} %param.11, pred[16,16]{1,0:T(8,128)(4,1)S(1)} %iota_compare_fusion), kind=kLoop, calls=%fused_computation.1 | loop fusion | flops 2976 | bytes 1024 | tf_op jit(solution)/shard_map/reduce_sum | solution.py:327
  2.3 0.1 copy.28
  2.4 0.7 %pad_clamp_fusion = s32[1024]{0:T(1024)S(1)} fusion(s32[8]{0:T(128)} %constant.36), kind=kLoop, calls=%fused_computation.4 | loop fusion | flops 1024 | bytes 4128 | tf_op jit(solution)/shard_map/gather | solution.py:330
  3.1 0.6 gather_fusion
  3.7 0.1 copy.29
  3.8 0.1 add_select_fusion
  3.9 0.1 copy.31
  4.0 0.1 broadcast_in_dim.47
  4.1 0.1 reshape.91
  4.2 0.6 %pad.9.bias_ref = f32[9,8,128]{2,1,0:T(8,128)} pad(f32[9,6,128]{2,1,0:T(8,128)S(1)} %reshape.91, f32[]{:T(128)} %constant.22.clone.1), padding=0_0x0_2x0_0 | pad | bytes 64516 | tf_op jit(solution)/shard_map/jit(_pad)/pad | solution.py:337
  4.8 1.3 %pad.8.new_ref = bf16[2,16,1024]{2,1,0:T(8,128)(2,1)} pad(bf16[2,4,1024]{2,1,0:T(4,128)(2,1)} %bitcast.23, bf16[]{:T(256)} %constant.9.clone.1), padding=0_0x0_12x0_0 | pad | bytes 81922 | tf_op jit(solution)/shard_map/jit(_pad)/pad | solution.py:325
  6.2 0.9 %copy.33 = bf16[1,4,128,128]{3,2,1,0:T(8,128)(2,1)S(1)} copy(bf16[1,4,128,128]{3,1,2,0:T(4,128)(2,1)} %bitcast.22) | data formatting | bytes 262144
  7.1 0.7 %copy.27 = bf16[4,8,16,128]{3,2,0,1:T(8,128)(2,1)} copy(bf16[4,8,16,128]{3,2,1,0:T(8,128)(2,1)S(1)} %bitcast.18) | data formatting | bytes 262144 | tf_op jit(solution)/shard_map/reshape | solution.py:324
  7.8 49.7 %shard_map.91 = bf16[8,64,128]{2,1,0:T(8,128)(2,1)} custom-call(bf16[8,64,128]{2,1,0:T(8,128)(2,1)} %bitcast.19, bf16[2,768,1024]{2,1,0:T(8,128)(2,1)} %kv_ref.1, bf16[2,256,1024]{2,1,0:T(8,128)(2,1)} %bitcast.17, bf16[2,16,1024]{2,1,0:T(8,128)(2,1)} %pad.8.new_ref, f32[9,8,128]{2,1,0:T(8,128)} %pad.9.bias_ref), custom_call_target="tpu_custom_call" | custom-call | tf_op jit(solution)/shard_map/pallas_call | solution.py:341
  57.5 0.9 %copy.32 = bf16[4,8,16,128]{3,2,1,0:T(8,128)(2,1)S(1)} copy(bf16[4,8,16,128]{3,2,0,1:T(8,128)(2,1)} %bitcast.20) | data formatting | bytes 262144 | tf_op jit(solution)/shard_map/transpose | solution.py:370
  58.4 0.7 %reshape.93 = bf16[1,4,16384]{2,1,0:T(4,128)(2,1)} reshape(bf16[4,8,16,128]{3,2,1,0:T(8,128)(2,1)S(1)} %copy.32) | data formatting | bytes 262144 | tf_op jit(solution)/shard_map/reshape | solution.py:371
  (4 shorter events, 0.0 us)

commit v2 on v1

--- a/solution.py
+++ b/solution.py
@@ -56,8 +56,8 @@
 
 
 def kernel(
-    chips, tokens, q_ref, kv_ref, suf_ref, new_ref, bias_ref, out_ref,
-    qb, kvs, sufs, news, bias, vt, svt, part_o, part_l, rs_in, rs_out, rl_in, rl_out, fin, land,
+    chips, tokens, q_ref, kv_ref, suf_ref, new_ref, mask_ref, slot_ref, live_ref, out_ref,
+    qb, kvs, sufs, news, fresh, bias, vt, svt, part_o, part_l, rs_in, rs_out, rl_in, rl_out, fin, land,
     loc_sem, sib_send, sib_recv, g_send, g_recv, o_send, o_recv, l_send, l_recv, f_send, f_recv,
 ):
     half = chips // 2
@@ -66,10 +66,12 @@
     odd, pair_no = lax.rem(chip, 2), lax.div(chip, 2)
     pos = (1 - odd) * pair_no + odd * (chips - 1 - pair_no)
 
+    def chip_at(position):
+        back = lax.div(position, half)
+        return (1 - back) * 2 * position + back * (2 * (chips - 1 - position) + 1)
+
     def at(position):
-        back = lax.div(position, half)
-        place = (1 - back) * 2 * position + back * (2 * (chips - 1 - position) + 1)
-        return {"node": place * 2 + core}
+        return {"node": chip_at(position) * 2 + core}
 
     sibling = {"node": node + 1 - 2 * core}
     ahead = (at(lax.rem(pos + 1, chips)), at(lax.rem(pos + chips - 1, chips)))
@@ -85,10 +87,9 @@
     def views(columns, heads):
         return (
             (q_ref.at[pl.ds(heads, HALF)], qb.at[pos, :, slot_rows, :]),
-            (bias_ref, bias.at[core]),
             (kv_ref.at[:, :, pl.ds(columns, HALF * DH)], kvs.at[:, core]),
             (suf_ref.at[:, :, pl.ds(columns, HALF * DH)], sufs.at[:, core]),
-            (new_ref.at[:, :, pl.ds(columns, HALF * DH)], news.at[:, core]),
+            (fresh.at[:, :, pl.ds(columns, HALF * DH)], news.at[:, core]),
         )
 
     local = [
@@ -132,11 +133,39 @@
             ),
         )
 
-    for copy in local:
+    across.append(
+        pltpu.make_async_remote_copy(
+            src_ref=bias.at[core], dst_ref=bias.at[core], send_sem=sib_send.at[4],
+            recv_sem=sib_recv.at[4], device_id=sibling,
+        )
+    )
+    for copy in local[:3]:
         copy.start()
     barrier = pltpu.get_barrier_semaphore()
     for other in (sibling, *ahead):
         pl.semaphore_signal(barrier, inc=1, device_id=other)
+    place16 = lax.broadcasted_iota(jnp.int32, (16, STEPS), 0)
+    pick = (place16 == lax.broadcasted_iota(jnp.int32, (16, STEPS), 1)).astype(BF16)
+    for i in range(2):
+        fresh[i] = jnp.dot(pick, new_ref[i], preferred_element_type=F32).astype(BF16)
+    requests, slots = mask_ref.shape[1], slot_ref.shape[1]
+    held = lax.broadcasted_iota(jnp.int32, (requests, slots), 0) == slot_ref[...]
+    visible = jnp.dot(
+        mask_ref[...].astype(F32), held.astype(F32), preferred_element_type=F32
+    )
+
+    @pl.loop(0, chips)
+    def _(b):
+        slot = lax.broadcasted_iota(jnp.int32, (slots, LANES), 0)
+        side = lax.div(lax.broadcasted_iota(jnp.int32, (slots, LANES), 1), ROWS)
+        spread = (slot == 2 * chip_at(b) + side).astype(F32)
+        seen = jnp.dot(visible, spread, preferred_element_type=F32)
+        bias[core, b] = jnp.where(seen > 0.5, 0.0, BIG)
+
+    page_row = lax.broadcasted_iota(jnp.int32, (pages, LANES), 0)
+    page_side = lax.div(lax.broadcasted_iota(jnp.int32, (pages, LANES), 1), ROWS)
+    bias[core, chips] = jnp.where((page_row < live_ref[0]) & (page_side == core), 0.0, BIG)
+    local[3].start()
     pl.semaphore_wait(barrier, 3)
     for copy in across:
         copy.start()
@@ -145,6 +174,17 @@
     for piece in range(2):
         for d in range(2):
             hop(d, 1, piece).start()
+
+    def pass_on(h):
+        for piece in range(2):
+            for d in range(2):
+                landed(d, h, piece).wait_recv()
+
+                @pl.when((h + 1 < half) | (d == piece))
+                def _():
+                    hop(d, h + 1, piece).start()
+
+    pass_on(1)
     for copy in local[1:]:
         copy.wait()
     for copy in across[1:]:
@@ -208,18 +248,6 @@
             keep(a, k, o[:, :LANES], lse[:, :LANES])
             keep(b, k, o[:, LANES:], lse[:, LANES:])
 
-    def pass_on(h):
-        for piece in range(2):
-            for d in range(2):
-                landed(d, h, piece).wait_recv()
-
-                @pl.when((h + 1 < half) | (d == piece))
-                def _():
-                    hop(d, h + 1, piece).start()
-
-    pass_on(1)
-    own_block()
-
     @pl.loop(2, half + 1)
     def _(h):
         @pl.when(h < half)
@@ -274,6 +302,8 @@
                     pl.when(j == 2)(begin)
                 for copy in stage(d, j, piece):
                     copy.start()
+
+        pl.when(j == 2)(own_block)
 
     for piece in range(2):
         for d in range(2):
@@ -309,46 +339,31 @@
                         copy.wait_send()
 
 
-def ring_order(chips):
-    return np.array([2 * r if r < chips // 2 else 2 * (chips - 1 - r) + 1 for r in range(chips)])
-
-
 def per_device(queries, shared_kv, page_mask, slot_request, suffix_blocks, suffix_kv, new_kv):
     nodes = lax.axis_size("node")
     chips = nodes // 2
     half = chips // 2
     tokens = shared_kv.shape[1]
     suffix_tokens = suffix_kv.shape[2]
-    core = lax.rem(lax.axis_index("node"), 2)
+    pages = page_mask.shape[0]
 
     q = queries.reshape(STEPS, KVH, G, DH).transpose(1, 0, 2, 3).reshape(KVH, ROWS, DH)
-    new = jnp.pad(new_kv[0], ((0, 0), (0, 16 - STEPS), (0, 0)))
-    selector = (slot_request[:, None] == jnp.arange(page_mask.shape[1])[None, :])
-    visible = jnp.sum(
-        jnp.where(selector[None], page_mask[:, None, :], 0), axis=-1
-    )
-    blocks = visible.reshape(-1, chips, 2)[:, ring_order(chips), :].transpose(1, 0, 2)
-    suffix_live = (jnp.arange(blocks.shape[1]) < suffix_blocks[0])[:, None] & (
-        jnp.arange(2) == core
-    )[None, :]
-    allowed = jnp.concatenate([blocks > 0, suffix_live[None]], axis=0)
-    bias = jnp.where(allowed, 0.0, BIG).astype(F32)
-    bias = jnp.repeat(bias, ROWS, axis=-1)
-    bias = jnp.pad(bias, ((0, 0), (0, -bias.shape[1] % 8), (0, 0)))
-
     dma = pltpu.SemaphoreType.DMA
     grid_sems = dma((2, half + 1, 2))
     out = pl.pallas_call(
         functools.partial(kernel, chips, tokens),
         out_shape=jax.ShapeDtypeStruct((KVH, ROWS, DH), BF16),
-        in_specs=[pl.BlockSpec(memory_space=pl.ANY)] * 5,
+        in_specs=[pl.BlockSpec(memory_space=pl.ANY)] * 3
+        + [pl.BlockSpec(memory_space=pltpu.VMEM)] * 3
+        + [pl.BlockSpec(memory_space=pltpu.SMEM)],
         out_specs=pl.BlockSpec(memory_space=pltpu.VMEM),
         scratch_shapes=[
             pltpu.VMEM((chips, HALF, LANES, DH), BF16),
             pltpu.VMEM((2, 2, tokens, HALF * DH), BF16),
             pltpu.VMEM((2, 2, suffix_tokens, HALF * DH), BF16),
             pltpu.VMEM((2, 2, 16, HALF * DH), BF16),
-            pltpu.VMEM((2,) + bias.shape, F32),
+            pltpu.VMEM((2, 16, KVH * DH), BF16),
+            pltpu.VMEM((2, chips + 1, pages, LANES), F32),
             pltpu.VMEM((HALF, 2, DH, tokens), BF16),
             pltpu.VMEM((HALF, 2, DH, suffix_tokens), BF16),
             pltpu.VMEM((chips, HALF, DH, LANES), F32),
@@ -359,14 +374,14 @@
             pltpu.VMEM((2, half + 1, 2, 8, LANES), F32),
             pltpu.VMEM((HALF, LANES, DH), BF16),
             pltpu.VMEM((HALF, ROWS, DH), BF16),
-            dma((5,)), dma((5,)), dma((5,)),
+            dma((4,)), dma((5,)), dma((5,)),
             grid_sems, grid_sems, grid_sems, grid_sems, grid_sems, grid_sems,
             dma, dma,
         ],
         compiler_params=pltpu.CompilerParams(
             collective_id=0, has_side_effects=True, vmem_limit_bytes=56 * 1024 * 1024
         ),
-    )(q, shared_kv, suffix_kv[0], new, bias)
+    )(q, shared_kv, suffix_kv[0], new_kv[0], page_mask, slot_request[None, :], suffix_blocks)
     out = out.reshape(KVH, STEPS, G, DH).transpose(1, 0, 2, 3)
     return out.reshape(1, STEPS, H * DH)
 

time: 59.4 us -> 54.1 us (0.911)
  local copies, waits for them, and re-layouts: 6.27 us -> 3.2 us
  other arithmetic: 2.44 us -> 0 us
    pad x2 -> x0, local copies, waits for them, and re-layouts: 1.96 us -> none  [the longest x1 1.34 us: per_device(): new = jnp.pad(new_kv[0], ((0, 0), (0, 16 - STEPS), (0, 0)))]
    reduce_sum x1 -> x0, other arithmetic: 0.86 us -> none  [per_device(): jnp.sum(jnp.where(selector[None], page_mask[:, None, :], 0), axis=-1)]
    eq x2 -> x0, other arithmetic: 0.74 us -> none  [the longest x1 0.73 us: per_device(): selector = slot_request[:, None] == jnp.arange(page_mask.shape[1])[None, :]]
    gather x1 -> x0, other arithmetic: 0.67 us -> none  [per_device(): visible.reshape(-1, chips, 2)[:, ring_order(chips), :].transpose(1, 0, 2)]
    gather x2 -> x0, local copies, waits for them, and re-layouts: 0.67 us -> none  [per_device(): visible.reshape(-1, chips, 2)[:, ring_order(chips), :].transpose(1, 0, 2)]
where the time goes in v2:
time: 54.1 us; the launch traced here: 53.9 us
  Pallas kernels  50 us (92%)
  local copies, waits for them, and re-layouts  3.2 us (6%)
  between operations  0.67 us (1%)
    pallas_call x1, Pallas kernels, per_device(): pl.pallas_call(functools.partial(kernel, chips, tokens), out_shape=jax.Sh...  50 us

profile of v2, /device:TPU:0, one launch (start us, length us, event | category | flops | bytes accessed | tf_op | source)
XLA Modules:
  0.0 53.9 jit_solution(3878597679021914627)
XLA Ops:
  0.7 0.9 %copy.10 = bf16[1,4,128,128]{3,2,1,0:T(8,128)(2,1)S(1)} copy(bf16[1,4,128,128]{3,1,2,0:T(4,128)(2,1)} %bitcast.19) | data formatting | bytes 262144
  1.6 0.7 %copy.8 = bf16[4,8,16,128]{3,2,0,1:T(8,128)(2,1)} copy(bf16[4,8,16,128]{3,2,1,0:T(8,128)(2,1)S(1)} %bitcast.18) | data formatting | bytes 262144 | tf_op jit(solution)/shard_map/reshape | solution.py:350
  2.2 50.0 %shard_map.73 = bf16[8,64,128]{2,1,0:T(8,128)(2,1)} custom-call(bf16[8,64,128]{2,1,0:T(8,128)(2,1)} %bitcast.16, bf16[2,768,1024]{2,1,0:T(8,128)(2,1)} %kv_ref.1, bf16[2,256,1024]{2,1,0:T(8,128)(2,1)} %bitcast.15, bf16[2,4,1024]{2,1,0:T(4,128)(2,1)} %bitcast.20, s32[6,16]{1,0:T(8,128)} %mask_ref.1, s32[1,16]{1,0:T(1,128)} %bitcast.21, s32[1]{0:T(128)S(6)} %copy.11.live_ref), custom_call_target="tpu_custom_call" | custom-call | tf_op jit(solution)/shard_map/pallas_call | solution.py:353
  52.3 0.9 %copy.9 = bf16[4,8,16,128]{3,2,1,0:T(8,128)(2,1)S(1)} copy(bf16[4,8,16,128]{3,2,0,1:T(8,128)(2,1)} %bitcast.17) | data formatting | bytes 262144 | tf_op jit(solution)/shard_map/transpose | solution.py:385
  53.2 0.7 %reshape.15 = bf16[1,4,16384]{2,1,0:T(4,128)(2,1)} reshape(bf16[4,8,16,128]{3,2,1,0:T(8,128)(2,1)S(1)} %copy.9) | data formatting | bytes 262144 | tf_op jit(solution)/shard_map/reshape | solution.py:386

commit v3 on v2

--- a/solution.py
+++ b/solution.py
@@ -144,6 +144,15 @@
     barrier = pltpu.get_barrier_semaphore()
     for other in (sibling, *ahead):
         pl.semaphore_signal(barrier, inc=1, device_id=other)
+    pl.semaphore_wait(barrier, 3)
+    for copy in across[:3]:
+        copy.start()
+    local[0].wait()
+    across[0].wait_recv()
+    for piece in range(2):
+        for d in range(2):
+            hop(d, 1, piece).start()
+
     place16 = lax.broadcasted_iota(jnp.int32, (16, STEPS), 0)
     pick = (place16 == lax.broadcasted_iota(jnp.int32, (16, STEPS), 1)).astype(BF16)
     for i in range(2):
@@ -166,15 +175,8 @@
     page_side = lax.div(lax.broadcasted_iota(jnp.int32, (pages, LANES), 1), ROWS)
     bias[core, chips] = jnp.where((page_row < live_ref[0]) & (page_side == core), 0.0, BIG)
     local[3].start()
-    pl.semaphore_wait(barrier, 3)
-    for copy in across:
+    for copy in across[3:]:
         copy.start()
-    local[0].wait()
-    across[0].wait_recv()
-    for piece in range(2):
-        for d in range(2):
-            hop(d, 1, piece).start()
-
     def pass_on(h):
         for piece in range(2):
             for d in range(2):
@@ -215,9 +217,9 @@
     def own_block():
         token = lax.broadcasted_iota(jnp.int32, (16, LANES), 0)
         lane = lax.broadcasted_iota(jnp.int32, (16, LANES), 1)
-        step = lax.rem(lax.div(lane, G), STEPS)
-
-        @pl.loop(0, HALF)
+        step = lax.rem(lane, STEPS)
+
+        @pl.loop(0, HALF, unroll=4)
         def _(k):
             found = shared_segments(k, [pos])
             for s in range(2):
@@ -236,12 +238,12 @@
             keep(pos, k, *attend(qb[pos, k], found))
 
     def one_block(block):
-        @pl.loop(0, HALF)
+        @pl.loop(0, HALF, unroll=4)
         def _(k):
             keep(block, k, *attend(qb[block, k], shared_segments(k, [block])))
 
     def two_blocks(a, b):
-        @pl.loop(0, HALF)
+        @pl.loop(0, HALF, unroll=4)
         def _(k):
             q = jnp.concatenate([qb[a, k], qb[b, k]], axis=0)
             o, lse = attend(q, shared_segments(k, [a, b]))
@@ -259,12 +261,12 @@
             for d in range(2):
                 landed(d, half, d).wait_recv()
             far = behind(0, half)
-            one_block(far)
             for d in range(2):
                 for i in range(2):
                     k = 2 * d + i
-                    rs_out[d, 1, k] = part_o[far, k].astype(BF16)
-                    rl_out[d, 1, d, i : i + 1, :] = part_l[far, k]
+                    o, lse = attend(qb[far, k], shared_segments(k, [far]))
+                    rs_out[d, 1, k] = o.astype(BF16)
+                    rl_out[d, 1, d, i : i + 1, :] = lse
                 for copy in stage(d, 1, d):
                     copy.start()
 
@@ -347,7 +349,7 @@
     suffix_tokens = suffix_kv.shape[2]
     pages = page_mask.shape[0]
 
-    q = queries.reshape(STEPS, KVH, G, DH).transpose(1, 0, 2, 3).reshape(KVH, ROWS, DH)
+    q = queries.reshape(STEPS, H, DH).transpose(1, 0, 2).reshape(KVH, ROWS, DH)
     dma = pltpu.SemaphoreType.DMA
     grid_sems = dma((2, half + 1, 2))
     out = pl.pallas_call(
@@ -382,7 +384,7 @@
             collective_id=0, has_side_effects=True, vmem_limit_bytes=56 * 1024 * 1024
         ),
     )(q, shared_kv, suffix_kv[0], new_kv[0], page_mask, slot_request[None, :], suffix_blocks)
-    out = out.reshape(KVH, STEPS, G, DH).transpose(1, 0, 2, 3)
+    out = out.reshape(H, STEPS, DH).transpose(1, 0, 2)
     return out.reshape(1, STEPS, H * DH)
 
 

time: 54.1 us -> 45.1 us (0.83)
  Pallas kernels: 50 us -> 42.6 us
  local copies, waits for them, and re-layouts: 3.2 us -> 1.61 us
    pallas_call x1, Pallas kernels: 50 us -> 42.6 us  [per_device(): pl.pallas_call(functools.partial(kernel, chips, tokens), out_shape=jax.Sh...]
    reshape x2 -> x0, local copies, waits for them, and re-layouts: 1.37 us -> none  [the longest x1 0.7 us: per_device(): return out.reshape(1, STEPS, H * DH)]
    transpose x1 -> x0, local copies, waits for them, and re-layouts: 0.91 us -> none  [per_device(): out = out.reshape(KVH, STEPS, G, DH).transpose(1, 0, 2, 3)]
    unnamed x1, local copies, waits for them, and re-layouts: 0.92 us -> 1.61 us
where the time goes in v3:
time: 45.1 us; the launch traced here: 44.9 us
  Pallas kernels  42.6 us (94%)
  local copies, waits for them, and re-layouts  1.61 us (4%)
  between operations  0.66 us (1%)
    pallas_call x1, Pallas kernels, per_device(): pl.pallas_call(functools.partial(kernel, chips, tokens), out_shape=jax.Sh...  42.6 us
    unnamed x1, local copies, waits for them, and re-layouts  1.61 us

profile of v3, /device:TPU:0, one launch (start us, length us, event | category | flops | bytes accessed | tf_op | source)
XLA Modules:
  0.0 44.9 jit_solution(3775811793175704431)
XLA Ops:
  0.7 42.6 %shard_map.73 = bf16[8,64,128]{2,1,0:T(8,128)(2,1)} custom-call(bf16[8,64,128]{2,1,0:T(8,128)(2,1)} %bitcast.15, bf16[2,768,1024]{2,1,0:T(8,128)(2,1)} %kv_ref.1, bf16[2,256,1024]{2,1,0:T(8,128)(2,1)} %bitcast.13, bf16[2,4,1024]{2,1,0:T(4,128)(2,1)} %bitcast.16, s32[6,16]{1,0:T(8,128)} %mask_ref.1, s32[1,16]{1,0:T(1,128)} %bitcast.17, s32[1]{0:T(128)S(6)} %copy.11.live_ref), custom_call_target="tpu_custom_call" | custom-call | tf_op jit(solution)/shard_map/pallas_call | solution.py:355
  43.3 1.6 %copy.12 = bf16[1,4,16384]{2,1,0:T(4,128)(2,1)} copy(bf16[1,4,16384]{2,1,0:T(4,128)(2,1)} %bitcast.14) | data formatting | bytes 262144

commit v4 on v3

--- a/solution.py
+++ b/solution.py
@@ -270,7 +270,11 @@
                 for copy in stage(d, 1, d):
                     copy.start()
 
-        two_blocks(behind(0, h - 1), behind(1, h - 1))
+        @pl.when(h != half - 1)
+        def _():
+            two_blocks(behind(0, h - 1), behind(1, h - 1))
+
+        pl.when(h == half - 1)(own_block)
 
     def incoming(d, j, piece):
         for copy in stage(d, j, piece):
@@ -305,7 +309,9 @@
                 for copy in stage(d, j, piece):
                     copy.start()
 
-        pl.when(j == 2)(own_block)
+        @pl.when(j == 2)
+        def _():
+            two_blocks(behind(0, half - 2), behind(1, half - 2))
 
     for piece in range(2):
         for d in range(2):

time: 45.1 us -> 44.7 us (level)
  no operation moved by 1% of the time
where the time goes in v4:
time: 44.7 us; the launch traced here: 44.5 us
  Pallas kernels  42.3 us (95%)
  local copies, waits for them, and re-layouts  1.61 us (4%)
  between operations  0.66 us (1%)
    pallas_call x1, Pallas kernels, per_device(): pl.pallas_call(functools.partial(kernel, chips, tokens), out_shape=jax.Sh...  42.3 us
    unnamed x1, local copies, waits for them, and re-layouts  1.61 us

profile of v4, /device:TPU:0, one launch (start us, length us, event | category | flops | bytes accessed | tf_op | source)
XLA Modules:
  0.0 44.5 jit_solution(16800991665989898864)
XLA Ops:
  0.7 42.3 %shard_map.73 = bf16[8,64,128]{2,1,0:T(8,128)(2,1)} custom-call(bf16[8,64,128]{2,1,0:T(8,128)(2,1)} %bitcast.15, bf16[2,768,1024]{2,1,0:T(8,128)(2,1)} %kv_ref.1, bf16[2,256,1024]{2,1,0:T(8,128)(2,1)} %bitcast.13, bf16[2,4,1024]{2,1,0:T(4,128)(2,1)} %bitcast.16, s32[6,16]{1,0:T(8,128)} %mask_ref.1, s32[1,16]{1,0:T(1,128)} %bitcast.17, s32[1]{0:T(128)S(6)} %copy.11.live_ref), custom_call_target="tpu_custom_call" | custom-call | tf_op jit(solution)/shard_map/pallas_call | solution.py:361
  42.9 1.6 %copy.12 = bf16[1,4,16384]{2,1,0:T(4,128)(2,1)} copy(bf16[1,4,16384]{2,1,0:T(4,128)(2,1)} %bitcast.14) | data formatting | bytes 262144
